TPU v7x, 256 devices: a whole 4x4x8 slice. The times are simulated.
256 devices in a mesh: rows: 64 (over y, x, z_lo, core), feat: 4 (over z_hi).
Axes of the slice: x: 4, y: 4, z: 8 (z_hi: 4, z_lo: 2; z = z_hi * 2 + z_lo), core: 2. Of those that a mesh axis runs over, the one named last changes fastest.
Arguments:
- cells: bfloat16 [4096, 128, 192], P('rows', 'feat'), may hold values from -6 to 6
- labels: int32 [4096], P('rows'), may hold values from 0 to 1, as said below
- missing: int32 [4096, 128], P('rows', 'feat'), may hold values 0 or 1
- feat_qkv: bfloat16 [192, 576], replicated, may hold values from -16 to 16
- feat_out: bfloat16 [192, 192], replicated, may hold values from -0.4375 to 0.4375
- gain_feat: float32 [192], replicated, may hold values from 0.25 to 1.75
- row_q: bfloat16 [192, 192], replicated, may hold values from -16 to 16
- row_kv: bfloat16 [192, 384], replicated, may hold values from -0.4375 to 0.4375
- row_out: bfloat16 [192, 192], replicated, may hold values from -0.4375 to 0.4375
- gain_row: float32 [192], replicated, may hold values from 0.25 to 1.75
- mlp_in: bfloat16 [192, 384], replicated, may hold values from -0.4375 to 0.4375
- mlp_out: bfloat16 [384, 192], replicated, may hold values from -0.3125 to 0.3125
- gain_mlp: float32 [192], replicated, may hold values from 0.25 to 1.75
Outputs:
- cells_out: bfloat16 [4096, 128, 192], P('rows', 'feat')
Inputs may be any that keep to these rules, and one draw needn't show every extreme that they name: `labels`: 1 marks a training row; each aligned block of 64 rows holds between 4 and 8 training rows, and some block holds exactly 8.
All inputs are finite; a program needn't handle non-finite values. No bound on the sum of `missing` on one device may be relied on, other than what follows from the above.
Results may differ from a plain program's by a relative error of at most 0.02.
The roundings to bfloat16 on the way count: a program that leaves them out, or rounds other values in their place, can miss the bound.
Values may be sent and summed in bfloat16 or wider, within the bound.
No kernel may reach another device: no remote copies, remote signals or barrier semaphores. Data moves between devices by JAX's collectives and lax.ppermute only.
A program may use at most 320 MiB of HBM per device.

v0:
```python
import math

import jax
import jax.numpy as jnp
from jax import lax
from jax.sharding import PartitionSpec as P

HEADS = 6
TRAIN_MOST = 8


EPSILON = 1e-05


def layer_norm(values, gain):
    average = jnp.mean(values, axis=-1, keepdims=True)
    centred = values - average
    variance = jnp.mean(centred * centred, axis=-1, keepdims=True)
    return centred * lax.rsqrt(variance + EPSILON) * gain


def feature_block(block_cells, block_absent, feat_qkv, feat_out, gain_feat):
    row_count, feats, width = block_cells.shape
    head_size = width // HEADS
    flattened = block_cells.reshape(row_count * feats, width)
    packed = jnp.dot(flattened, feat_qkv, preferred_element_type=jnp.float32).astype(jnp.bfloat16)
    packed = packed.reshape(row_count, feats, 3, HEADS, head_size)
    scores = jnp.einsum(
        "bihd,bjhd->bhij", packed[:, :, 0], packed[:, :, 1], preferred_element_type=jnp.float32
    ) / math.sqrt(head_size)
    diagonal = jnp.eye(feats, dtype=bool)
    allowed = (block_absent[:, None, None, :] == 0) | diagonal[None, None]
    scores = jnp.where(allowed, scores, -jnp.inf)
    highest = jnp.max(scores, axis=-1, keepdims=True)
    weights = jnp.exp(scores - highest)
    summed = jnp.sum(weights, axis=-1)
    attended = jnp.einsum(
        "bhij,bjhd->bihd",
        weights.astype(jnp.bfloat16),
        packed[:, :, 2],
        preferred_element_type=jnp.float32,
    )
    attended = attended / jnp.transpose(summed, (0, 2, 1))[..., None]
    attended = attended.astype(jnp.bfloat16).reshape(row_count * feats, width)
    merged = flattened.astype(jnp.float32) + jnp.dot(
        attended, feat_out, preferred_element_type=jnp.float32
    )
    return layer_norm(merged, gain_feat).astype(jnp.bfloat16).reshape(row_count, feats, width)


def local(
    cells,
    labels,
    missing,
    feat_qkv,
    feat_out,
    gain_feat,
    row_q,
    row_kv,
    row_out,
    gain_row,
    mlp_in,
    mlp_out,
    gain_mlp,
):
    rows_dev, feats_dev, width = cells.shape
    head_size = width // HEADS
    row_cells, absent = (
        lax.all_to_all(cells, "feat", split_axis=0, concat_axis=1, tiled=True),
        lax.all_to_all(
            missing.astype(jnp.bfloat16), "feat", split_axis=0, concat_axis=1, tiled=True
        ),
    )
    row_count, all_feats = (row_cells.shape[0], row_cells.shape[1])
    row_group = math.gcd(row_count, 8)

    def feature_step(operands):
        return feature_block(operands[0], operands[1], feat_qkv, feat_out, gain_feat)

    feature_rows = lax.map(
        feature_step,
        (
            row_cells.reshape(row_count // row_group, row_group, all_feats, width),
            absent.reshape(row_count // row_group, row_group, all_feats),
        ),
    )
    feature_rows = feature_rows.reshape(row_count, all_feats, width)
    after_features = lax.all_to_all(feature_rows, "feat", split_axis=1, concat_axis=0, tiled=True)
    flattened = after_features.reshape(rows_dev * feats_dev, width)
    block_feats = math.gcd(feats_dev, 2)
    block_count = feats_dev // block_feats
    queries = jnp.dot(flattened, row_q, preferred_element_type=jnp.float32).astype(jnp.bfloat16)
    queries = queries.reshape(rows_dev, block_count, block_feats, HEADS, head_size).transpose(
        1, 2, 3, 0, 4
    )
    slot_index = jnp.cumsum(labels) - 1
    positions = jnp.arange(TRAIN_MOST, dtype=jnp.int32)
    select = ((slot_index[None, :] == positions[:, None]) & (labels[None, :] == 1)).astype(
        jnp.bfloat16
    )
    chosen = jnp.dot(
        select,
        after_features.reshape(rows_dev, feats_dev * width),
        preferred_element_type=jnp.float32,
    )
    chosen = chosen.astype(jnp.bfloat16).reshape(TRAIN_MOST, feats_dev, width)
    occupied = (positions < jnp.sum(labels)).astype(jnp.bfloat16)
    start_carry = (
        jnp.full((block_count, block_feats, HEADS, rows_dev), -jnp.inf, jnp.float32),
        jnp.zeros((block_count, block_feats, HEADS, rows_dev), jnp.float32),
        jnp.zeros((block_count, block_feats, HEADS, rows_dev, head_size), jnp.float32),
    )
    projected = jnp.dot(
        chosen.reshape(TRAIN_MOST * feats_dev, width), row_kv, preferred_element_type=jnp.float32
    )
    projected = projected.astype(jnp.bfloat16).reshape(TRAIN_MOST, feats_dev, 2 * width)
    keyvals = lax.all_gather(projected, "rows", axis=0, tiled=True)
    occupied_piece = lax.all_gather(occupied, "rows", axis=0, tiled=True)
    piece_rows = keyvals.shape[0]
    shaped = keyvals.reshape(piece_rows, block_count, block_feats, 2, HEADS, head_size)
    key_part = shaped[:, :, :, 0].transpose(1, 2, 3, 0, 4)
    value_part = shaped[:, :, :, 1].transpose(1, 2, 3, 0, 4)

    def attend_block(operands):
        query_block, key_block, value_block, highest, summed, accumulated = operands
        scores = jnp.einsum(
            "fhrd,fhnd->fhrn", query_block, key_block, preferred_element_type=jnp.float32
        ) / math.sqrt(head_size)
        scores = jnp.where(occupied_piece[None, None, None, :] > 0, scores, -jnp.inf)
        new_highest = jnp.maximum(highest, jnp.max(scores, axis=-1))
        offset = jnp.where(jnp.isinf(new_highest), 0.0, new_highest)
        weights = jnp.exp(scores - offset[..., None])
        rescale = jnp.exp(highest - offset)
        summed = summed * rescale + jnp.sum(weights, axis=-1)
        contribution = jnp.einsum(
            "fhrn,fhnd->fhrd",
            weights.astype(jnp.bfloat16),
            value_block,
            preferred_element_type=jnp.float32,
        )
        accumulated = accumulated * rescale[..., None] + contribution
        return (new_highest, summed, accumulated)

    highest, summed, accumulated = lax.map(
        attend_block, (queries, key_part, value_part) + tuple(start_carry)
    )
    attended = accumulated / summed[..., None]
    attended = (
        attended.transpose(3, 0, 1, 2, 4).reshape(rows_dev * feats_dev, width).astype(jnp.bfloat16)
    )
    merged = flattened.astype(jnp.float32) + jnp.dot(
        attended, row_out, preferred_element_type=jnp.float32
    )
    after_rows = layer_norm(merged, gain_row).astype(jnp.bfloat16)
    hidden = jax.nn.gelu(jnp.dot(after_rows, mlp_in, preferred_element_type=jnp.float32)).astype(
        jnp.bfloat16
    )
    combined = after_rows.astype(jnp.float32) + jnp.dot(
        hidden, mlp_out, preferred_element_type=jnp.float32
    )
    return layer_norm(combined, gain_mlp).astype(jnp.bfloat16).reshape(rows_dev, feats_dev, width)


def solution(mesh):
    placed = (
        P("rows", "feat", None),
        P("rows"),
        P("rows", "feat"),
        P(),
        P(),
        P(),
        P(),
        P(),
        P(),
        P(),
        P(),
        P(),
        P(),
    )
    return jax.shard_map(
        local, mesh=mesh, in_specs=placed, out_specs=P("rows", "feat", None), check_vma=False
    )
```

profile of v0, /device:TPU:1, one launch (start us, length us, event | category | flops | bytes accessed | tf_op | source)
XLA Modules:
  0.0 373.0 jit_solution(1379880790279619790)
XLA Ops:
  6.5 0.8 copy.67
  7.5 15.4 %all_to_all.46 = bf16[4,2,256]{2,1,0:T(2,128)(2,1)S(1)} all-to-all(bf16[4,2,256]{2,1,0:T(2,128)(2,1)S(1)} %reshape.200), channel_id=1, replica_groups=mesh['rows'=64,'feat'=4] {'feat'}, dimensions={0} | all-to-all | bytes 8192 | tf_op jit(solution)/shard_map/all_to_all | solution.py:70
  22.8 3.5 all-to-all-start
  26.6 23.1 %all-to-all-done = bf16[64,32,192]{2,1,0:T(8,128)(2,1)S(1)} async-done(((bf16[64,32,192]{2,1,0:T(8,128)(2,1)}), bf16[64,32,192]{2,1,0:T(8,128)(2,1)S(1)}, u32[]{:S(2)}, u32[]{:S(2)}) %all-to-all-start) | async-done | bytes 786464 | tf_op jit(solution)/shard_map/all_to_all | solution.py:69
  49.8 0.7 copy.69
  51.0 9.5 %while.22 = (s32[]{:T(128)}, bf16[2,8,128,192]{2,3,1,0:T(8,128)(2,1)S(1)}, bf16[2,8,128,192]{2,1,3,0:T(8,128)(2,1)S(1)}, bf16[192,576]{1,0:T(8,128)(2,1)S(1)}, b...) while((s32[]{:T(128)}, ...), condition=%wide.region_5.6_spmd, body=%wide.region_0.5_spmd.sunk | while | flops 414390272 | bytes 25002848 | solution.py:80
  52.3 0.8 fusion.109
  53.0 0.9 fusion.110
  53.9 0.8 fusion.111
  57.0 0.8 fusion.109
  57.8 0.9 fusion.110
  58.7 0.8 fusion.111
  60.6 1.7 copy.71
  62.2 5.2 %all-to-all-start.2 = ((bf16[16,128,192]{2,0,1:T(8,128)(2,1)}), bf16[16,128,192]{2,0,1:T(8,128)(2,1)S(1)}, u32[]{:S(2)}, u32[]{:S(2)}) async-start(bf16[16,128,192]{2,0,1:T(8,128)(2,1)} %copy.71), calls=%async_computation.2 | async-start | bytes 2097152 | tf_op jit(solution)/shard_map/all_to_all | solution.py:88
  67.7 17.7 %all-to-all-done.2 = bf16[16,128,192]{2,0,1:T(8,128)(2,1)S(1)} async-done(((bf16[16,128,192]{2,0,1:T(8,128)(2,1)}), bf16[16,128,192]{2,0,1:T(8,128)(2,1)S(1)}, u32[]{:S(2)}, u32[]{:S(2)}) %all-to-all-start.2) | async-done | bytes 786464 | tf_op jit(solution)/shard_map/all_to_all | solution.py:88
  85.9 1.1 reshape.190
  87.4 0.9 convolution_convert_fusion.3
  88.4 0.7 reduce_sum.83
  89.0 0.6 dynamic-slice
  91.2 148.7 %all-reduce = bf16[512]{0:T(512)(128)(2,1)S(1)} all-reduce(bf16[512]{0:T(512)(128)(2,1)S(1)} %dynamic-update-slice), channel_id=1, replica_groups=mesh['rows'=64,'feat'=4] {'rows'}, use_global_device_ids=true, to_apply=%add | all-reduce | flops 512 | bytes 2048
  241.4 3.5 reshape.188
  245.0 5.0 %copy.79 = bf16[16,2,6,64,32]{3,4,2,1,0:T(8,128)(2,1)S(1)} copy(bf16[16,2,6,64,32]{4,2,1,0,3:T(8,128)(2,1)} %bitcast.179) | data formatting | bytes 1572864 | tf_op jit(solution)/shard_map/while | solution.py:144
  250.0 16.9 %copy.78 = bf16[512,32,384]{0,2,1:T(8,128)(2,1)} copy(bf16[512,32,384]{2,1,0:T(8,128)(2,1)} %all-gather.2.cloned.1.call-done) | data formatting | bytes 25165824 | tf_op jit(solution)/shard_map/all_gather | solution.py:117
  266.9 10.7 %slice_bitcast_fusion = (bf16[16,2,6,512,32]{3,4,2,1,0:T(8,128)(2,1)}, bf16[16,2,6,512,32]{3,4,2,1,0:T(8,128)(2,1)}) fusion(bf16[512,16,2,2,6,32]{0,5,4,3,2,1:T(8,128)(2,1)} %bitcast.176), kind=kLoop, calls=%fused_computation.65 | loop fusion | bytes 25165824 | tf_op jit(solution)/shard_map/transpose | solution.py:122
  277.6 68.0 %while.23 = (s32[]{:T(128)}, f32[16,2,6,64]{3,2,1,0:T(8,128)S(1)}, f32[16,2,6,64,32]{3,4,2,1,0:T(8,128)}, bf16[512]{0:T(512)(128)(2,1)S(1)}, bf16[16,2,6,64,32]{...) while((s32[]{:T(128)}, f32[16,2,6,64]{3,2,1,0:T(8,128)S(1)}, ...), condition=%wide.region_11.12_spmd, body=%wide.region_8.11_spmd.sunk | while | flops 53116160 | bytes 5853273 | solution.py:144
  277.6 1.5 fusion.116
  279.1 2.1 fusion.119
  281.9 1.5 fusion.116
  283.4 2.1 fusion.119
  286.1 1.5 fusion.116
  287.6 2.1 fusion.119
  290.4 1.5 fusion.116
  291.9 2.1 fusion.119
  294.6 1.5 fusion.116
  296.1 2.1 fusion.119
  298.9 1.5 fusion.116
  300.4 2.1 fusion.119
  303.1 1.5 fusion.116
  304.6 2.1 fusion.119
  307.4 1.5 fusion.116
  308.9 2.1 fusion.119
  311.6 1.5 fusion.116
  313.1 2.1 fusion.119
  315.9 1.5 fusion.116
  317.4 2.1 fusion.119
  320.1 1.5 fusion.116
  321.6 2.1 fusion.119
  324.3 1.5 fusion.116
  325.9 2.1 fusion.119
  328.6 1.5 fusion.116
  330.1 2.1 fusion.119
  332.8 1.5 fusion.116
  334.4 2.1 fusion.119
  337.1 1.5 fusion.116
  338.6 2.1 fusion.119
  341.3 1.5 fusion.116
  342.9 2.1 fusion.119
  345.6 2.4 fusion.55
  348.0 6.9 %copy.80 = bf16[64,16,2,6,32]{4,3,2,1,0:T(8,128)(2,1)} copy(bf16[64,16,2,6,32]{0,4,3,2,1:T(8,128)(2,1)S(1)} %fusion.55) | data formatting | bytes 1572864 | tf_op jit(solution)/shard_map/convert_element_type | solution.py:149
  354.9 5.0 %convert_element_type.66 = bf16[2048,192]{1,0:T(8,128)(2,1)S(1)} reshape(bf16[64,16,2,6,32]{4,3,2,1,0:T(8,128)(2,1)} %copy.80) | data formatting | bytes 1572864 | tf_op jit(solution)/shard_map/convert_element_type | solution.py:149
  359.9 1.4 fusion.73
  361.6 0.7 copy-done.9
  362.3 1.7 fusion.74
  364.9 1.3 copy.81
  (149 shorter events, 19.4 us)
Async XLA Ops:
  6.5 355.1 %copy-start = (bf16[384,192]{0,1:T(8,128)(2,1)S(1)}, bf16[384,192]{0,1:T(8,128)(2,1)}, u32[]{:S(2)}) copy-start(bf16[384,192]{0,1:T(8,128)(2,1)} %param.28) | copy-start | bytes 442372
  22.8 26.8 %all-to-all-start = ((bf16[64,32,192]{2,1,0:T(8,128)(2,1)}), bf16[64,32,192]{2,1,0:T(8,128)(2,1)S(1)}, u32[]{:S(2)}, u32[]{:S(2)}) async-start(bf16[64,32,192]{2,1,0:T(8,128)(2,1)} %param.17), calls=%async_computation | async-start | bytes 2097152 | tf_op jit(solution)/shard_map/all_to_all | solution.py:69
  49.7 0.9 copy-start.1
  49.7 1.0 copy-start.2
  49.7 1.0 copy-start.6
  49.8 1.3 copy-start.3
  60.6 6.9 %copy-start.8 = (s32[64]{0:T(128)S(1)}, s32[64]{0:T(128)}, u32[]{:S(2)}) copy-start(s32[64]{0:T(128)} %param.18) | copy-start | bytes 772
  62.2 23.2 %all-to-all-start.2 = ((bf16[16,128,192]{2,0,1:T(8,128)(2,1)}), bf16[16,128,192]{2,0,1:T(8,128)(2,1)S(1)}, u32[]{:S(2)}, u32[]{:S(2)}) async-start(bf16[16,128,192]{2,0,1:T(8,128)(2,1)} %copy.71), calls=%async_computation.2 | async-start | bytes 2097152 | tf_op jit(solution)/shard_map/all_to_all | solution.py:88
  67.4 182.6 %all-gather.2.cloned.1.call-start = ((), (), s32[]{:S(2)}) async-start(), calls=%async_computation.3 | async-start | bytes 12779520 | tf_op jit(solution)/shard_map/all_gather | solution.py:117
  85.8 1.6 copy-start.4
  85.8 3.2 copy-start.11
  87.2 153.2 %copy-start.5 = (bf16[192,192]{1,0:T(8,128)(2,1)S(1)}, bf16[192,192]{1,0:T(8,128)(2,1)}, u32[]{:S(2)}) copy-start(bf16[192,192]{1,0:T(8,128)(2,1)} %param.23) | copy-start | bytes 221188
  361.4 0.9 copy-start.9
  361.4 0.9 copy-start.10
  364.0 0.7 copy-start.7
Sparse Core Ops, SparseCore 0:
  88.5 128.6 all-gather.1
where the time goes:
time: 376 us; the launch traced here: 373 us
  blocking collectives  164 us (44%)
  matrix products  67.4 us (18%)
  local copies, waits for them, and re-layouts  60.1 us (16%)
  waiting for transfers between devices  40.9 us (11%)
  other arithmetic  16.7 us (4%)
  between operations  14.4 us (4%)
  starting transfers between devices  8.69 us (2%)
    unnamed x1, blocking collectives  149 us
    dot_general x16, matrix products, attend_block(): jnp.einsum('fhrn,fhnd->fhrd', weights.astype(jnp.bfloat16), value_block,...  33.8 us
    dot_general x16, matrix products, attend_block(): jnp.einsum('fhrd,fhnd->fhrn', query_block, key_block, preferred_element_t...  24 us
    all_to_all x1, waiting for transfers between devices, local(): lax.all_to_all(cells, 'feat', split_axis=0, concat_axis=1, tiled=True)  23.1 us
    all_to_all x1, waiting for transfers between devices, local(): lax.all_to_all(feature_rows, 'feat', split_axis=1, concat_axis=0, tiled=T...  17.7 us
    all_gather x1, local copies, waits for them, and re-layouts, local(): keyvals = lax.all_gather(projected, 'rows', axis=0, tiled=True)  16.9 us
    all_to_all x1, blocking collectives, local(): lax.all_to_all(missing.astype(jnp.bfloat16), 'feat', split_axis=0, concat...  15.4 us
    convert_element_type x2, local copies, waits for them, and re-layouts, local(): attended.transpose(3, 0, 1, 2, 4).reshape(rows_dev * feats_dev, width)  11.9 us
  transfers between devices with their start and end apart: 3, of which 2 were waited for; matrix products, arithmetic and copies ran while one was open for 3% of the time, Pallas kernels for 0%

commit v1 on v0

v1 whole, which is shorter than its diff:
```python
import functools
import math

import jax
import jax.numpy as jnp
from jax import lax
from jax.experimental import pallas as pl
from jax.experimental.pallas import tpu as pltpu
from jax.sharding import PartitionSpec as P

HEADS = 6
HEAD = 32
WIDTH = 192
TAIL = WIDTH - 128
TRAIN_MOST = 8
EPSILON = 1e-05
BF = jnp.bfloat16
F32 = jnp.float32
NEVER = -1e30
SCALE = math.log2(math.e) / math.sqrt(HEAD)
VMEM = pl.BlockSpec(memory_space=pltpu.VMEM)
SMEM = pl.BlockSpec(memory_space=pltpu.SMEM)


def mm(a, b):
    return lax.dot_general(a, b, (((1,), (0,)), ((), ())), preferred_element_type=F32)


def mm_nt(a, b):
    return lax.dot_general(a, b, (((1,), (1,)), ((), ())), preferred_element_type=F32)


def mm_tn(a, b):
    return lax.dot_general(a, b, (((0,), (0,)), ((), ())), preferred_element_type=F32)


def layer_norm(values, gain):
    average = jnp.mean(values, axis=-1, keepdims=True)
    centred = values - average
    variance = jnp.mean(centred * centred, axis=-1, keepdims=True)
    return centred * lax.rsqrt(variance + EPSILON) * gain


def turned(w):
    return jnp.transpose(w.astype(F32)).astype(BF)


def params(flops, size, exps=0):
    return dict(
        compiler_params=pltpu.CompilerParams(vmem_limit_bytes=56 * 2**20),
        cost_estimate=pl.CostEstimate(flops=flops, bytes_accessed=size, transcendentals=exps),
    )


def halves(tail, part):
    return tail[:, part * TAIL : (part + 1) * TAIL]


def prepare_kernel(rows_dev, feats, cells, labels, missing, out0, out1, out2, out3, train, picked, flags):
    me = lax.axis_index("feat")
    share = rows_dev // 4
    count = share * feats
    for k, out in enumerate((out0, out1, out2, out3)):
        start = lax.rem(me + k, 4) * share
        x = cells[pl.ds(start, share)].reshape(count, WIDTH)
        out[0:count, :] = x[:, :128]
        out[count : count + count // 2, 0:TAIL] = x[: count // 2, 128:]
        out[count : count + count // 2, TAIL:128] = x[count // 2 :, 128:]
        out[count * 3 // 2 :, :] = jnp.zeros((share, 128), BF)
        out[count * 3 // 2 :, 0:feats] = missing[pl.ds(start, share), :].astype(F32).astype(BF)
    picked[...] = jnp.zeros(picked.shape, BF)
    flags[...] = jnp.zeros(flags.shape, F32)

    def step(r, slot):
        is_train = labels[r] == 1

        @pl.when(is_train)
        def _():
            picked[slot] = cells[r]
            flags[pl.ds(slot, 1), 0:feats] = missing[pl.ds(r, 1), :].astype(F32)

        return jnp.minimum(slot + is_train.astype(jnp.int32), TRAIN_MOST - 1)

    lax.fori_loop(0, rows_dev, step, jnp.int32(0))
    count = TRAIN_MOST * feats
    x = picked[...].reshape(count, WIDTH)
    train[0:count, :] = x[:, :128]
    train[count : count + count // 2, 0:TAIL] = x[: count // 2, 128:]
    train[count : count + count // 2, TAIL:128] = x[count // 2 :, 128:]
    train[count * 3 // 2 :, :] = flags[...].astype(BF)


def feature_rows(pieces, rows, feats, weights, scratch, keep, emit):
    feat_qkv, feat_out, gain_feat = weights
    turned_qv, blocks = scratch
    all_feats = 4 * feats
    turned_qv[0:WIDTH, :] = turned(feat_qkv[:, 0:WIDTH])
    turned_qv[WIDTH : 2 * WIDTH, :] = turned(feat_qkv[:, 2 * WIDTH : 3 * WIDTH])
    blocks[...] = jnp.zeros(blocks.shape, BF)
    count = rows * feats
    flags = jnp.concatenate([p[count * 3 // 2 :, 0:feats].astype(F32) for p in pieces], axis=1)
    flags = jnp.concatenate(
        [flags, jnp.zeros((128 - flags.shape[0], all_feats), F32)], axis=0
    )
    flags = jnp.transpose(flags)
    same = lax.broadcasted_iota(jnp.int32, (all_feats, all_feats), 0) == lax.broadcasted_iota(
        jnp.int32, (all_feats, all_feats), 1
    )
    gain = gain_feat[...]
    for r in range(rows // 2):
        pair = []
        for part in range(2):
            row = r + part * (rows // 2)
            pair.extend(
                jnp.concatenate(
                    [
                        p[row * feats : (row + 1) * feats, :],
                        halves(p[count + r * feats : count + (r + 1) * feats, :], part),
                    ],
                    axis=1,
                )
                for p in pieces
            )
        x = jnp.concatenate(pair, axis=0)
        keys = mm(x, feat_qkv[:, WIDTH : 2 * WIDTH]).astype(BF)
        turned_q_v = mm_nt(turned_qv[...], x).astype(BF)
        for part in range(2):
            row = r + part * (rows // 2)
            lanes = slice(part * all_feats, (part + 1) * all_feats)
            spot = blocks.at[part]
            for h in range(HEADS):
                spot[h * HEAD : (h + 1) * HEAD, h * 128 : h * 128 + 128] = turned_q_v[
                    h * HEAD : (h + 1) * HEAD, lanes
                ]
            allowed = (flags[:, row : row + 1] == 0) | same
            attended = []
            for g in range(HEADS // 2):
                scores = mm(keys[lanes, :], spot[:, g * 256 : (g + 1) * 256])
                scores = jnp.concatenate(
                    [jnp.where(allowed, scores[:, i * 128 : (i + 1) * 128], NEVER) for i in range(2)],
                    axis=1,
                )
                highest = jnp.max(scores, axis=0, keepdims=True)
                exps = jnp.exp2((scores - highest) * SCALE)
                total = jnp.sum(exps, axis=0, keepdims=True)
                mixed = mm(
                    turned_q_v[WIDTH + g * 64 : WIDTH + (g + 1) * 64, lanes], exps.astype(BF)
                )
                attended.append((mixed[0:HEAD, 0:128] / total[:, 0:128]).astype(BF))
                attended.append((mixed[HEAD:64, 128:256] / total[:, 128:256]).astype(BF))
            attended = jnp.concatenate(attended, axis=0)
            update = mm_tn(attended, feat_out[...])[0:keep]
            merged = x[part * all_feats : part * all_feats + keep].astype(F32) + update
            emit(row, layer_norm(merged, gain))


def train_kernel(
    feats, p0, p1, p2, p3, labels, feat_qkv, feat_out, gain_feat, mine, other, turned_qv, blocks, heads, tails
):
    core = lax.rem(lax.axis_index("rows"), 2)

    def emit(row, y):
        heads[pl.ds(row, feats, stride=TRAIN_MOST), :] = y[:, :128]
        tails[pl.ds(row, feats, stride=TRAIN_MOST), :] = jnp.concatenate([y[:, 128:], y[:, 128:]], axis=1)

    feature_rows(
        (p0, p1, p2, p3), TRAIN_MOST, feats, (feat_qkv, feat_out, gain_feat), (turned_qv, blocks), feats, emit
    )
    count = feats // 2 * TRAIN_MOST
    trained = jnp.sum(labels[...], axis=1, keepdims=True)
    bias = jnp.where(lax.broadcasted_iota(jnp.int32, (16, 128), 0) < trained, 0.0, NEVER)
    for rel, out in enumerate((mine, other)):
        base = jnp.where(rel == 0, core, 1 - core) * count
        out[0:count, :] = heads[pl.ds(base, count), :].astype(BF)
        first = tails[pl.ds(base, count // 2), 0:TAIL]
        second = tails[pl.ds(base + count // 2, count // 2), TAIL:128]
        out[count : count * 3 // 2, :] = jnp.concatenate([first, second], axis=1).astype(BF)
        out[count * 3 // 2 :, :] = bias.astype(BF)


def merge_kernel(feats, a, b, c, d, out):
    count = feats * TRAIN_MOST
    parts = [p[...].astype(F32) for p in (a, b, c, d)]

    def side(start, groups):
        joined = jnp.concatenate(
            [p[start : start + groups * 8].reshape(groups, 8, 128) for p in parts], axis=1
        )
        return joined.reshape(groups * 32, 128).astype(BF)

    out[0 : 4 * count, :] = side(0, feats)
    out[4 * count : 6 * count, :] = side(count, feats // 2)
    out[6 * count :, :] = side(count * 3 // 2, 1)


def feature_kernel(
    rows,
    feats,
    p0,
    p1,
    p2,
    p3,
    feat_qkv,
    feat_out,
    gain_feat,
    *rest,
):
    outs, (turned_qv, blocks, heads, tails) = rest[:8], rest[8:]
    core = lax.rem(lax.axis_index("rows"), 2)

    def emit(row, y):
        heads[pl.ds(row, 4 * feats, stride=rows), :] = y[:, :128]
        tails[pl.ds(row, 4 * feats, stride=rows), :] = jnp.concatenate([y[:, 128:], y[:, 128:]], axis=1)

    feature_rows(
        (p0, p1, p2, p3), rows, feats, (feat_qkv, feat_out, gain_feat), (turned_qv, blocks), 4 * feats, emit
    )
    count = feats // 2 * rows
    for k in range(4):
        for rel in range(2):
            base = (2 * k + jnp.where(rel == 0, core, 1 - core)) * count
            out = outs[2 * k + rel]
            out[0:count, :] = heads[pl.ds(base, count), :].astype(BF)
            first = tails[pl.ds(base, count // 2), 0:TAIL]
            second = tails[pl.ds(base + count // 2, count // 2), TAIL:128]
            out[count:, :] = jnp.concatenate([first, second], axis=1).astype(BF)


def row_kernel(feats, share, train_each, *refs):
    trains, chunks = refs[0:4], refs[4:12]
    row_q, row_kv, row_out, gain_row, mlp_in, mlp_out, gain_mlp = refs[12:19]
    mine, other = refs[19:21]
    turned_q, turned_v, blocks, train_cells, row_cells, bias, heads, tails = refs[21:]
    rows = share * len(chunks)
    piece = feats * train_each * 3 // 2 + train_each
    lines = trains[0].shape[0] // piece
    keys_all = 4 * lines * train_each
    turned_q[...] = turned(row_q[...])
    turned_v[...] = turned(row_kv[:, WIDTH : 2 * WIDTH])
    blocks[...] = jnp.zeros(blocks.shape, BF)
    blocks[:, WIDTH : WIDTH + 16, :] = jnp.where(
        lax.broadcasted_iota(jnp.int32, (2, 16, HEADS * 128), 1) == 0, 1.0, 0.0
    ).astype(BF)
    for n in range(4):
        for line in range(lines):
            spot = (n * lines + line) * train_each
            bias[spot : spot + train_each, :] = trains[n][
                line * piece + feats * train_each * 3 // 2 : (line + 1) * piece, 0:TAIL
            ]

    def pair(j, carry):
        for n in range(4):
            for line in range(lines):
                spot = slice((n * lines + line) * train_each, (n * lines + line + 1) * train_each)
                base = line * piece
                tail = trains[n][
                    pl.ds(base + feats * train_each + j * train_each, train_each), :
                ]
                for part in range(2):
                    train_cells[part, spot, 0:128] = trains[n][
                        pl.ds(base + (j + part * (feats // 2)) * train_each, train_each), :
                    ]
                    train_cells[part, spot, 128:WIDTH] = halves(tail, part)
        for n, chunk in enumerate(chunks):
            tail = chunk[pl.ds(feats * share + j * share, share), :]
            for part in range(2):
                spot = slice(part * rows + n * share, part * rows + (n + 1) * share)
                row_cells[spot, 0:128] = chunk[pl.ds((j + part * (feats // 2)) * share, share), :]
                row_cells[spot, 128:WIDTH] = halves(tail, part)
        x = row_cells[...]
        turned_queries = mm_nt(turned_q[...], x).astype(BF)
        updates = []
        for part in range(2):
            cells = train_cells[part]
            keys = jnp.concatenate([mm(cells, row_kv[:, 0:WIDTH]).astype(BF), bias[...]], axis=1)
            values = mm_nt(turned_v[...], cells).astype(BF)
            spot = blocks.at[part]
            for h in range(HEADS):
                spot[h * HEAD : (h + 1) * HEAD, h * 128 : h * 128 + 128] = turned_queries[
                    h * HEAD : (h + 1) * HEAD, part * rows : (part + 1) * rows
                ]
            attended = []
            for g in range(HEADS // 2):
                scores = mm(keys, spot[:, g * 256 : (g + 1) * 256])
                highest = jnp.max(scores, axis=0, keepdims=True)
                exps = jnp.exp2((scores - highest) * SCALE)
                total = jnp.sum(exps, axis=0, keepdims=True)
                mixed = mm(values[g * 64 : (g + 1) * 64, :], exps.astype(BF))
                attended.append((mixed[0:HEAD, 0:128] / total[:, 0:128]).astype(BF))
                attended.append((mixed[HEAD:64, 128:256] / total[:, 128:256]).astype(BF))
            updates.append(mm_tn(jnp.concatenate(attended, axis=0), row_out[...]))
        merged = x.astype(F32) + jnp.concatenate(updates, axis=0)
        after_rows = layer_norm(merged, gain_row[...]).astype(BF)
        hidden = jax.nn.gelu(mm(after_rows, mlp_in[...])).astype(BF)
        combined = after_rows.astype(F32) + mm(hidden, mlp_out[...])
        y = layer_norm(combined, gain_mlp[...])
        for part in range(2):
            own = y[part * rows : (part + 1) * rows]
            spot = pl.ds(j + part * (feats // 2), rows, stride=feats)
            heads[spot, :] = own[:, :128]
            tails[spot, :] = jnp.concatenate([own[:, 128:], own[:, 128:]], axis=1)
        return carry

    lax.fori_loop(0, feats // 2, pair, 0)
    count = rows // 2 * feats
    for rel, out in enumerate((mine, other)):
        out[0:count, :] = heads[rel * count : (rel + 1) * count, :].astype(BF)
        first = tails[rel * count : rel * count + count // 2, 0:TAIL]
        second = tails[rel * count + count // 2 : (rel + 1) * count, TAIL:128]
        out[count:, :] = jnp.concatenate([first, second], axis=1).astype(BF)


def finish_kernel(rows, feats, mine, theirs, out):
    me = lax.axis_index("feat")
    core = lax.rem(lax.axis_index("rows"), 2)
    share = rows // 4
    count = rows * feats

    def whole(ref, k):
        n = share * feats
        part = k // 2
        tail = ref[count + (k % 2) * n : count + (k % 2 + 1) * n, :]
        x = jnp.concatenate([ref[k * n : (k + 1) * n, :], halves(tail, part)], axis=1)
        return x.reshape(share, feats, WIDTH)

    for first in range(2):

        @pl.when(core == first)
        def _():
            for k in range(4):
                start = lax.rem(me + k, 4) * share
                out[pl.ds(start, share), first * feats : (first + 1) * feats, :] = whole(mine, k)
                out[pl.ds(start, share), (1 - first) * feats : (2 - first) * feats, :] = whole(theirs, k)


def spot_of(y, x, z, c):
    return ((y * 4 + x) * 2 + z) * 2 + c


def moves(change):
    return [
        (spot_of(y, x, z, c), spot_of(*change(y, x, z, c)))
        for y in range(4)
        for x in range(4)
        for z in range(2)
        for c in range(2)
    ]


def moves_both(change):
    return [
        (spot_of(y, x, z, c) * 4 + f, (lambda t: spot_of(*t[0]) * 4 + t[1])(change((y, x, z, c), f)))
        for y in range(4)
        for x in range(4)
        for z in range(2)
        for c in range(2)
        for f in range(4)
    ]


def along(shift, first):
    def change(y, x, z, c):
        if (c == 0) == first:
            return (y, (x + shift) % 4, z, c)
        return ((y + shift) % 4, x, z, c)

    return moves(change)


def local(
    cells,
    labels,
    missing,
    feat_qkv,
    feat_out,
    gain_feat,
    row_q,
    row_kv,
    row_out,
    gain_row,
    mlp_in,
    mlp_out,
    gain_mlp,
):
    rows, feats, width = cells.shape
    share = rows // 4
    half = feats // 2
    gain_feat, gain_row, gain_mlp = (g.reshape(1, width) for g in (gain_feat, gain_row, gain_mlp))

    def shape(n):
        return jax.ShapeDtypeStruct((n, 128), BF)

    main_n = share * feats * 3 // 2 + share
    train_n = TRAIN_MOST * feats * 3 // 2 + 16
    *mains, train = pl.pallas_call(
        functools.partial(prepare_kernel, rows, feats),
        out_shape=[shape(main_n)] * 4 + [shape(train_n)],
        in_specs=[VMEM, SMEM, VMEM],
        out_specs=[VMEM] * 5,
        scratch_shapes=[pltpu.VMEM((TRAIN_MOST, feats, width), BF), pltpu.VMEM((16, 128), F32)],
        name="prepare",
        **params(0, 2 * cells.size * 2),
    )(cells, labels, missing)

    def turn(array, k):
        return lax.ppermute(array, "feat", [(f, (f + k) % 4) for f in range(4)])

    trains = [train] + [turn(train, k) for k in (1, 2, 3)]
    *trains, mains = lax.optimization_barrier((*trains, tuple(mains)))
    mains = [mains[0]] + [turn(mains[k], k) for k in (1, 2, 3)]

    weights = (feat_qkv, feat_out, gain_feat)
    scratch = [pltpu.VMEM((2 * width, width), BF), pltpu.VMEM((2, width, HEADS * 128), BF)]
    piece_n = half * TRAIN_MOST * 3 // 2 + 16
    own, away = pl.pallas_call(
        functools.partial(train_kernel, feats),
        out_shape=[shape(piece_n)] * 2,
        in_specs=[VMEM] * 8,
        out_specs=[VMEM] * 2,
        scratch_shapes=scratch
        + [pltpu.VMEM((feats * TRAIN_MOST, 128), F32), pltpu.VMEM((feats * TRAIN_MOST, 128), F32)],
        name="train_rows",
        **params(2 * 10**9, 10**6, 10**6),
    )(*trains, labels.reshape(1, rows), *weights)
    near = [
        lax.ppermute(own, "rows", moves(lambda y, x, z, c: (y, x, 1 - z, c))),
        lax.ppermute(away, "rows", moves(lambda y, x, z, c: (y, x, z, 1 - c))),
        lax.ppermute(away, "rows", moves(lambda y, x, z, c: (y, x, 1 - z, 1 - c))),
    ]
    train_each = 4 * TRAIN_MOST
    group_n = half * train_each * 3 // 2 + train_each
    group = pl.pallas_call(
        functools.partial(merge_kernel, half),
        out_shape=shape(group_n),
        in_specs=[VMEM] * 4,
        out_specs=VMEM,
        name="merge",
        **params(0, 10**6),
    )(own, *near)
    line = jnp.concatenate(
        [group] + [lax.ppermute(group, "rows", along(k, True)) for k in (1, 2, 3)], axis=0
    )
    plane = [line] + [lax.ppermute(line, "rows", along(k, False)) for k in (1, 2, 3)]

    chunk_n = half * share * 3 // 2
    pieces = pl.pallas_call(
        functools.partial(feature_kernel, share, feats),
        out_shape=[shape(chunk_n)] * 8,
        in_specs=[VMEM] * 7,
        out_specs=[VMEM] * 8,
        scratch_shapes=scratch
        + [pltpu.VMEM((4 * feats * share, 128), F32), pltpu.VMEM((4 * feats * share, 128), F32)],
        name="features",
        **params(4 * 10**9, 3 * 10**6, 2 * 10**6),
    )(*mains, *weights)

    def back(array, k, cross):
        def change(spot, f):
            y, x, z, c = spot
            return (y, x, z, c ^ cross), (f - k) % 4

        return lax.ppermute(array, ("rows", "feat"), moves_both(change))

    chunks = []
    for cross in range(2):
        for k in range(4):
            array = pieces[2 * k + cross]
            chunks.append(array if k == 0 and cross == 0 else back(array, k, cross))

    out_n = rows * half * 3 // 2
    mine, other = pl.pallas_call(
        functools.partial(row_kernel, half, share, train_each),
        out_shape=[shape(out_n)] * 2,
        in_specs=[VMEM] * 19,
        out_specs=[VMEM] * 2,
        scratch_shapes=[
            pltpu.VMEM((width, width), BF),
            pltpu.VMEM((width, width), BF),
            pltpu.VMEM((2, 256, HEADS * 128), BF),
            pltpu.VMEM((2, 16 * train_each, width), BF),
            pltpu.VMEM((4 * rows, width), BF),
            pltpu.VMEM((16 * train_each, TAIL), BF),
            pltpu.VMEM((2 * rows * half, 128), F32),
            pltpu.VMEM((2 * rows * half, 128), F32),
        ],
        name="rows",
        **params(20 * 10**9, 6 * 10**6, 7 * 10**6),
    )(*plane, *chunks, row_q, row_kv, row_out, gain_row, mlp_in, mlp_out, gain_mlp)
    theirs = lax.ppermute(other, "rows", moves(lambda y, x, z, c: (y, x, z, 1 - c)))
    return pl.pallas_call(
        functools.partial(finish_kernel, rows, half),
        out_shape=jax.ShapeDtypeStruct(cells.shape, BF),
        in_specs=[VMEM] * 2,
        out_specs=VMEM,
        name="finish",
        **params(0, 2 * 10**6),
    )(mine, theirs)


def solution(mesh):
    placed = (
        P("rows", "feat", None),
        P("rows"),
        P("rows", "feat"),
        P(),
        P(),
        P(),
        P(),
        P(),
        P(),
        P(),
        P(),
        P(),
        P(),
    )
    return jax.shard_map(
        local, mesh=mesh, in_specs=placed, out_specs=P("rows", "feat", None), check_vma=False
    )
```

time: 376 us -> 161 us (0.43)
  blocking collectives: 164 us -> 0 us
  matrix products: 67.4 us -> 0 us
  Pallas kernels: 0 us -> 65.5 us
  local copies, waits for them, and re-layouts: 60.1 us -> 6.96 us
  starting transfers between devices: 8.69 us -> 49.4 us
  other arithmetic: 16.7 us -> 0.98 us
  between operations: 14.4 us -> 0.1 us
  waiting for transfers between devices: 40.9 us -> 36.1 us
    unnamed x1 -> x0, blocking collectives: 149 us -> none
    dot_general x45 -> x0, matrix products: 67.4 us -> none  [the longest x16 33.8 us: attend_block(): jnp.einsum('fhrn,fhnd->fhrd', weights.astype(jnp.bfloat16), value_block,...]
    pallas_call x0 -> x6, Pallas kernels: none -> 65.5 us  [the longest x1 37.1 us: local(): pl.pallas_call(functools.partial(row_kernel, half, share, train_each), ou...]
    ppermute x0 -> x23, starting transfers between devices: none -> 49.4 us  [the longest x6 18.2 us: turn(): return lax.ppermute(array, 'feat', [(f, (f + k) % 4) for f in range(4)])]
    all_to_all x2 -> x0, waiting for transfers between devices: 40.8 us -> none  [the longest x1 23.1 us: local(): lax.all_to_all(cells, 'feat', split_axis=0, concat_axis=1, tiled=True)]
    ppermute x0 -> x23, waiting for transfers between devices: none -> 36.1 us  [the longest x6 17.6 us: turn(): return lax.ppermute(array, 'feat', [(f, (f + k) % 4) for f in range(4)])]
    all_gather x1 -> x0, local copies, waits for them, and re-layouts: 16.9 us -> none  [local(): keyvals = lax.all_gather(projected, 'rows', axis=0, tiled=True)]
    all_to_all x1 -> x0, blocking collectives: 15.4 us -> none  [local(): lax.all_to_all(missing.astype(jnp.bfloat16), 'feat', split_axis=0, concat...]
  transfers between devices with their start and end apart: 3 -> 23, of which waited for: 2 -> 11; matrix products, arithmetic and copies ran while one was open for 3% -> 1% of each run, Pallas kernels for 0% -> 9%
where the time goes in v1:
time: 161 us; the launch traced here: 159 us
  Pallas kernels  65.5 us (41%)
  starting transfers between devices  49.4 us (31%)
  waiting for transfers between devices  36.1 us (22%)
  local copies, waits for them, and re-layouts  6.96 us (4%)
    pallas_call x1, Pallas kernels, local(): pl.pallas_call(functools.partial(row_kernel, half, share, train_each), ou...  37.1 us
    ppermute x6, starting transfers between devices, turn(): return lax.ppermute(array, 'feat', [(f, (f + k) % 4) for f in range(4)])  18.2 us
    ppermute x7, starting transfers between devices, back(): return lax.ppermute(array, ('rows', 'feat'), moves_both(change))  17.9 us
    ppermute x6, waiting for transfers between devices, turn(): return lax.ppermute(array, 'feat', [(f, (f + k) % 4) for f in range(4)])  17.6 us
    pallas_call x1, Pallas kernels, local(): pl.pallas_call(functools.partial(feature_kernel, share, feats), out_shape...  14 us
    ppermute x7, waiting for transfers between devices, back(): return lax.ppermute(array, ('rows', 'feat'), moves_both(change))  13.8 us
    pallas_call x1, Pallas kernels, local(): pl.pallas_call(functools.partial(train_kernel, feats), out_shape=[shape(p...  7.27 us
    unnamed x40, local copies, waits for them, and re-layouts  6.96 us
  transfers between devices with their start and end apart: 23, of which 11 were waited for; matrix products, arithmetic and copies ran while one was open for 1% of the time, Pallas kernels for 9%

profile of v1, /device:TPU:1, one launch (start us, length us, event | category | flops | bytes accessed | tf_op | source)
XLA Modules:
  0.0 159.1 jit_solution(14411916059936150292)
XLA Ops:
  0.0 1.4 copy.14.missing
  1.4 3.3 %prepare.1 = (bf16[784,128]{1,0:T(8,128)(2,1)}, bf16[784,128]{1,0:T(8,128)(2,1)}, bf16[784,128]{1,0:T(8,128)(2,1)}, bf16[784,128]{1,0:T(8,128)(2,1)}, bf16[400,128]{1,0:T(8,128)(2,1)}) custom-call(bf16[64,32,192]{2,1,0:T(8,128)(2,1)} %cells.1, s32[64]{0:T(128)} %labels.1, s32[64,32]{1,0:T(8,128)} %copy.14.missing), custom_call_target="tpu_custom_call" | custom-call | bytes 1572864 | tf_op jit(solution)/shard_map/prepare/pallas_call | solution.py:395
  4.7 6.8 %collective-permute-start.2 = (bf16[400,128]{1,0:T(8,128)(2,1)}, bf16[400,128]{1,0:T(8,128)(2,1)S(1)}, u32[]{:S(2)}, u32[]{:S(2)}) collective-permute-start(bf16[400,128]{1,0:T(8,128)(2,1)} %get-tuple-element.35.p0), channel_id=1, source_target_pairs={{0,3},{1,0},{2,1},{3,2},{4,7},{5,4},{6,5},{7,6},{8,11},{9,8},{10,9... | collective-permute-start | bytes 307208 | tf_op jit(solution)/shard_map/ppermute | solution.py:406
  11.6 0.9 collective-permute-start.1
  12.5 2.3 %collective-permute-start = (bf16[400,128]{1,0:T(8,128)(2,1)}, bf16[400,128]{1,0:T(8,128)(2,1)S(1)}, u32[]{:S(2)}, u32[]{:S(2)}) collective-permute-start(bf16[400,128]{1,0:T(8,128)(2,1)} %get-tuple-element.35.p0), channel_id=1, source_target_pairs={{0,1},{1,2},{2,3},{3,0},{4,5},{5,6},{6,7},{7,4},{8,9},{9,10},{10,1... | collective-permute-start | bytes 307208 | tf_op jit(solution)/shard_map/ppermute | solution.py:406
  14.8 0.0 collective-permute-done.2.p3
  14.8 5.7 %collective-permute-done.1.p2 = bf16[400,128]{1,0:T(8,128)(2,1)S(1)} collective-permute-done((bf16[400,128]{1,0:T(8,128)(2,1)}, bf16[400,128]{1,0:T(8,128)(2,1)S(1)}, u32[]{:S(2)}, u32[]{:S(2)}) %collective-permute-start.1) | collective-permute-done | bytes 102432 | tf_op jit(solution)/shard_map/ppermute | solution.py:406
  20.5 0.4 collective-permute-done.p1
  20.9 0.3 copy-done.16
  21.2 0.4 copy-done.17
  21.5 7.3 %train_rows.1 = (bf16[208,128]{1,0:T(8,128)(2,1)}, bf16[208,128]{1,0:T(8,128)(2,1)}) custom-call(bf16[400,128]{1,0:T(8,128)(2,1)} %get-tuple-element.35.p0, bf16[400,128]{1,0:T(8,128)(2,1)} %copy-done.17, bf16[400,128]{1,0:T(8,128)(2,1)} %copy-done.16, bf16[400,128]{1,0:T(8,128)(2,1)} %copy-done.15, s32[1,64]{1,0:T(1,128)} %bitcast.4, ...), custom_call_target="tpu_custom_call" | custom-call | flops 2000000000 | bytes 1000000 | tf_op jit(solution)/shard_map/train_rows/pallas_call | solution.py:415
  28.8 3.2 %collective-permute-start.3 = (bf16[208,128]{1,0:T(8,128)(2,1)}, bf16[208,128]{1,0:T(8,128)(2,1)S(1)}, u32[]{:S(2)}, u32[]{:S(2)}) collective-permute-start(bf16[208,128]{1,0:T(8,128)(2,1)} %get-tuple-element.39.a), channel_id=1, source_target_pairs={{0,8},{4,12},{8,0},{12,4},{16,24},{20,28},{24,16},{28,20},{32,40},... | collective-permute-start | bytes 159752 | tf_op jit(solution)/shard_map/ppermute | solution.py:426
  32.0 2.4 %collective-permute-start.5 = (bf16[208,128]{1,0:T(8,128)(2,1)}, bf16[208,128]{1,0:T(8,128)(2,1)S(1)}, u32[]{:S(2)}, u32[]{:S(2)}) collective-permute-start(bf16[208,128]{1,0:T(8,128)(2,1)} %get-tuple-element.40), channel_id=1, source_target_pairs={{0,12},{4,8},{8,4},{12,0},{16,28},{20,24},{24,20},{28,16},{32,44},... | collective-permute-start | bytes 159752 | tf_op jit(solution)/shard_map/ppermute | solution.py:428
  34.3 0.0 collective-permute-start.4
  34.3 0.0 collective-permute-done.3.b
  34.3 3.2 %collective-permute-done.5.d = bf16[208,128]{1,0:T(8,128)(2,1)S(1)} collective-permute-done((bf16[208,128]{1,0:T(8,128)(2,1)}, bf16[208,128]{1,0:T(8,128)(2,1)S(1)}, u32[]{:S(2)}, u32[]{:S(2)}) %collective-permute-start.5) | collective-permute-done | bytes 53280 | tf_op jit(solution)/shard_map/ppermute | solution.py:428
  37.5 0.0 collective-permute-done.4.c
  37.5 0.6 copy-done.4
  38.1 0.6 copy-done.5
  38.7 1.6 %merge.1 = bf16[800,128]{1,0:T(8,128)(2,1)} custom-call(bf16[208,128]{1,0:T(8,128)(2,1)} %get-tuple-element.39.a, bf16[208,128]{1,0:T(8,128)(2,1)} %copy-done.3, bf16[208,128]{1,0:T(8,128)(2,1)} %copy-done.5, bf16[208,128]{1,0:T(8,128)(2,1)} %copy-done.4), custom_call_target="tpu_custom_call" | custom-call | bytes 1000000 | tf_op jit(solution)/shard_map/merge/pallas_call | solution.py:432
  40.3 2.5 %collective-permute-start.8 = (bf16[800,128]{1,0:T(8,128)(2,1)}, bf16[800,128]{1,0:T(8,128)(2,1)S(1)}, u32[]{:S(2)}, u32[]{:S(2)}) collective-permute-start(bf16[800,128]{1,0:T(8,128)(2,1)} %merge.1), channel_id=1, source_target_pairs={{0,48},{4,196},{8,56},{12,204},{16,0},{20,212},{24,8},{28,220},{32... | collective-permute-start | bytes 614408 | tf_op jit(solution)/shard_map/ppermute | solution.py:441
  42.9 0.3 collective-permute-start.7
  43.2 0.7 collective-permute-start.6
  43.9 1.0 collective-permute-start.12
  45.0 3.6 %collective-permute-start.13 = (bf16[784,128]{1,0:T(8,128)(2,1)S(1)}, bf16[784,128]{1,0:T(8,128)(2,1)S(1)}, u32[]{:S(2)}, u32[]{:S(2)}) collective-permute-start(bf16[784,128]{1,0:T(8,128)(2,1)S(1)} %copy-done.10), channel_id=1, source_target_pairs={{0,2},{1,3},{2,0},{3,1},{4,6},{5,7},{6,4},{7,5},{8,10},{9,11},{10,... | collective-permute-start | bytes 602120 | tf_op jit(solution)/shard_map/ppermute | solution.py:406
  48.5 3.5 %collective-permute-start.14 = (bf16[784,128]{1,0:T(8,128)(2,1)S(1)}, bf16[784,128]{1,0:T(8,128)(2,1)S(1)}, u32[]{:S(2)}, u32[]{:S(2)}) collective-permute-start(bf16[784,128]{1,0:T(8,128)(2,1)S(1)} %copy-done.9), channel_id=1, source_target_pairs={{0,3},{1,0},{2,1},{3,2},{4,7},{5,4},{6,5},{7,6},{8,11},{9,8},{10,9... | collective-permute-start | bytes 602120 | tf_op jit(solution)/shard_map/ppermute | solution.py:406
  52.0 0.0 collective-permute-done.7
  52.0 0.0 collective-permute-done.6
  52.0 1.0 pad_maximum_fusion.refs_0_
  53.0 0.0 copy-start
  53.0 0.0 copy-start.2
  53.0 2.7 %collective-permute-start.11 = (bf16[3200,128]{1,0:T(8,128)(2,1)S(1)}, bf16[3200,128]{1,0:T(8,128)(2,1)S(1)}, u32[]{:S(2)}, u32[]{:S(2)}) collective-permute-start(bf16[3200,128]{1,0:T(8,128)(2,1)S(1)} %pad_maximum_fusion.refs_0_), channel_id=1, source_target_pairs={{0,192},{4,52},{8,200},{12,60},{16,208},{20,4},{24,216},{28,12},{3... | collective-permute-start | bytes 2457608 | tf_op jit(solution)/shard_map/ppermute | solution.py:443
  55.8 0.5 collective-permute-start.10
  56.3 0.0 collective-permute-done.12.p1
  56.3 0.6 collective-permute-start.9
  56.9 0.5 collective-permute-done.13.p2
  57.4 11.1 %collective-permute-done.14.p3 = bf16[784,128]{1,0:T(8,128)(2,1)S(1)} collective-permute-done((bf16[784,128]{1,0:T(8,128)(2,1)S(1)}, bf16[784,128]{1,0:T(8,128)(2,1)S(1)}, u32[]{:S(2)}, u32[]{:S(2)}) %collective-permute-start.14) | collective-permute-done | bytes 200736 | tf_op jit(solution)/shard_map/ppermute | solution.py:406
  68.4 0.7 copy-done.14
  69.1 14.0 %features.1 = (bf16[384,128]{1,0:T(8,128)(2,1)}, bf16[384,128]{1,0:T(8,128)(2,1)}, bf16[384,128]{1,0:T(8,128)(2,1)}, bf16[384,128]{1,0:T(8,128)(2,1)}, bf16[384,...) custom-call(bf16[784,128]{1,0:T(8,128)(2,1)} %get-tuple-element.41.p0, ...), custom_call_target="tpu_custom_call" | custom-call | flops 4000000000 | bytes 3000000 | tf_op jit(solution)/shard_map/features/pallas_call | solution.py:446
  83.1 2.9 %collective-permute-start.15 = (bf16[384,128]{1,0:T(8,128)(2,1)}, bf16[384,128]{1,0:T(8,128)(2,1)S(1)}, u32[]{:S(2)}, u32[]{:S(2)}) collective-permute-start(bf16[384,128]{1,0:T(8,128)(2,1)} %get-tuple-element.46), channel_id=1, source_target_pairs={{0,3},{1,0},{2,1},{3,2},{4,7},{5,4},{6,5},{7,6},{8,11},{9,8},{10,9... | collective-permute-start | bytes 294920 | tf_op jit(solution)/shard_map/ppermute | solution.py:462
  86.0 1.7 %collective-permute-start.16 = (bf16[384,128]{1,0:T(8,128)(2,1)}, bf16[384,128]{1,0:T(8,128)(2,1)}, u32[]{:S(2)}, u32[]{:S(2)}) collective-permute-start(bf16[384,128]{1,0:T(8,128)(2,1)} %get-tuple-element.47), channel_id=1, source_target_pairs={{0,2},{1,3},{2,0},{3,1},{4,6},{5,7},{6,4},{7,5},{8,10},{9,11},{10,... | collective-permute-start | bytes 294920 | tf_op jit(solution)/shard_map/ppermute | solution.py:462
  87.7 2.7 %collective-permute-done.15.refs_5_ = bf16[384,128]{1,0:T(8,128)(2,1)S(1)} collective-permute-done((bf16[384,128]{1,0:T(8,128)(2,1)}, bf16[384,128]{1,0:T(8,128)(2,1)S(1)}, u32[]{:S(2)}, u32[]{:S(2)}) %collective-permute-start.15) | collective-permute-done | bytes 98336 | tf_op jit(solution)/shard_map/ppermute | solution.py:462
  90.4 3.0 %collective-permute-start.17 = (bf16[384,128]{1,0:T(8,128)(2,1)}, bf16[384,128]{1,0:T(8,128)(2,1)}, u32[]{:S(2)}, u32[]{:S(2)}) collective-permute-start(bf16[384,128]{1,0:T(8,128)(2,1)} %get-tuple-element.48), channel_id=1, source_target_pairs={{0,1},{1,2},{2,3},{3,0},{4,5},{5,6},{6,7},{7,4},{8,9},{9,10},{10,1... | collective-permute-start | bytes 294920 | tf_op jit(solution)/shard_map/ppermute | solution.py:462
  93.4 0.3 collective-permute-done.16.refs_6_
  93.7 2.0 %collective-permute-start.18 = (bf16[384,128]{1,0:T(8,128)(2,1)}, bf16[384,128]{1,0:T(8,128)(2,1)}, u32[]{:S(2)}, u32[]{:S(2)}) collective-permute-start(bf16[384,128]{1,0:T(8,128)(2,1)} %get-tuple-element.49), channel_id=1, source_target_pairs={{0,4},{1,5},{2,6},{3,7},{4,0},{5,1},{6,2},{7,3},{8,12},{9,13},{10,... | collective-permute-start | bytes 294920 | tf_op jit(solution)/shard_map/ppermute | solution.py:462
  95.8 0.5 collective-permute-done.17.refs_7_
  96.3 4.1 %collective-permute-start.19 = (bf16[384,128]{1,0:T(8,128)(2,1)}, bf16[384,128]{1,0:T(8,128)(2,1)}, u32[]{:S(2)}, u32[]{:S(2)}) collective-permute-start(bf16[384,128]{1,0:T(8,128)(2,1)} %get-tuple-element.50), channel_id=1, source_target_pairs={{0,7},{1,4},{2,5},{3,6},{4,3},{5,0},{6,1},{7,2},{8,15},{9,12},{10,... | collective-permute-start | bytes 294920 | tf_op jit(solution)/shard_map/ppermute | solution.py:462
  100.4 0.0 collective-permute-done.18.refs_8_
  100.4 2.1 %collective-permute-start.20 = (bf16[384,128]{1,0:T(8,128)(2,1)}, bf16[384,128]{1,0:T(8,128)(2,1)}, u32[]{:S(2)}, u32[]{:S(2)}) collective-permute-start(bf16[384,128]{1,0:T(8,128)(2,1)} %get-tuple-element.51), channel_id=1, source_target_pairs={{0,6},{1,7},{2,4},{3,5},{4,2},{5,3},{6,0},{7,1},{8,14},{9,15},{10,... | collective-permute-start | bytes 294920 | tf_op jit(solution)/shard_map/ppermute | solution.py:462
  102.5 4.6 %collective-permute-done.19.refs_9_ = bf16[384,128]{1,0:T(8,128)(2,1)} collective-permute-done((bf16[384,128]{1,0:T(8,128)(2,1)}, bf16[384,128]{1,0:T(8,128)(2,1)}, u32[]{:S(2)}, u32[]{:S(2)}) %collective-permute-start.19) | collective-permute-done | bytes 98336 | tf_op jit(solution)/shard_map/ppermute | solution.py:462
  107.1 2.0 %collective-permute-start.21 = (bf16[384,128]{1,0:T(8,128)(2,1)}, bf16[384,128]{1,0:T(8,128)(2,1)}, u32[]{:S(2)}, u32[]{:S(2)}) collective-permute-start(bf16[384,128]{1,0:T(8,128)(2,1)} %get-tuple-element.52), channel_id=1, source_target_pairs={{0,5},{1,6},{2,7},{3,4},{4,1},{5,2},{6,3},{7,0},{8,13},{9,14},{10,... | collective-permute-start | bytes 294920 | tf_op jit(solution)/shard_map/ppermute | solution.py:462
  109.1 0.8 copy.15.refs_17_
  109.9 0.0 collective-permute-done.20.refs_10_
  109.9 5.7 %collective-permute-done.21.refs_11_ = bf16[384,128]{1,0:T(8,128)(2,1)} collective-permute-done((bf16[384,128]{1,0:T(8,128)(2,1)}, bf16[384,128]{1,0:T(8,128)(2,1)}, u32[]{:S(2)}, u32[]{:S(2)}) %collective-permute-start.21) | collective-permute-done | bytes 98336 | tf_op jit(solution)/shard_map/ppermute | solution.py:462
  115.6 0.0 collective-permute-done.10.refs_2_
  115.6 0.0 collective-permute-done.9.refs_1_
  115.6 0.9 copy-done.6
  116.5 0.3 copy-done.7
  116.8 0.2 copy-done.8
  117.0 37.1 %rows.1 = (bf16[1536,128]{1,0:T(8,128)(2,1)}, bf16[1536,128]{1,0:T(8,128)(2,1)}) custom-call(bf16[3200,128]{1,0:T(8,128)(2,1)} %copy-done, bf16[3200,128]{1,0:T(8,128)(2,1)} %copy-done.8, bf16[3200,128]{1,0:T(8,128)(2,1)} %copy-done.7, bf16[3200,128]{1,0:T(8,128)(2,1)} %copy-done.6, bf16[384,128]{1,0:T(8,128)(2,1)} %get-tuple-element.45.refs_4_, ...), custom_call_target="tpu_custom_call" | custom-call | flops 20000000000 | bytes 6000000 | tf_op jit(solution)/shard_map/rows/pallas_call | solution.py:471
  154.2 0.4 collective-permute-start.22
  154.6 1.6 collective-permute-done.22.theirs
  156.1 0.7 copy-done.1
  156.9 2.2 %finish.1 = bf16[64,32,192]{2,1,0:T(8,128)(2,1)} custom-call(bf16[1536,128]{1,0:T(8,128)(2,1)} %get-tuple-element.53.mine, bf16[1536,128]{1,0:T(8,128)(2,1)} %copy-done.1), custom_call_target="tpu_custom_call" | custom-call | bytes 2000000 | tf_op jit(solution)/shard_map/finish/pallas_call | solution.py:490
  (29 shorter events, 0.1 us)
Async XLA Ops:
  4.7 10.1 %collective-permute-start.2 = (bf16[400,128]{1,0:T(8,128)(2,1)}, bf16[400,128]{1,0:T(8,128)(2,1)S(1)}, u32[]{:S(2)}, u32[]{:S(2)}) collective-permute-start(bf16[400,128]{1,0:T(8,128)(2,1)} %get-tuple-element.35.p0), channel_id=1, source_target_pairs={{0,3},{1,0},{2,1},{3,2},{4,7},{5,4},{6,5},{7,6},{8,11},{9,8},{10,9... | collective-permute-start | bytes 307208 | tf_op jit(solution)/shard_map/ppermute | solution.py:406
  11.6 8.9 %collective-permute-start.1 = (bf16[400,128]{1,0:T(8,128)(2,1)}, bf16[400,128]{1,0:T(8,128)(2,1)S(1)}, u32[]{:S(2)}, u32[]{:S(2)}) collective-permute-start(bf16[400,128]{1,0:T(8,128)(2,1)} %get-tuple-element.35.p0), channel_id=1, source_target_pairs={{0,2},{1,3},{2,0},{3,1},{4,6},{5,7},{6,4},{7,5},{8,10},{9,11},{10,... | collective-permute-start | bytes 307208 | tf_op jit(solution)/shard_map/ppermute | solution.py:406
  12.5 8.4 %collective-permute-start = (bf16[400,128]{1,0:T(8,128)(2,1)}, bf16[400,128]{1,0:T(8,128)(2,1)S(1)}, u32[]{:S(2)}, u32[]{:S(2)}) collective-permute-start(bf16[400,128]{1,0:T(8,128)(2,1)} %get-tuple-element.35.p0), channel_id=1, source_target_pairs={{0,1},{1,2},{2,3},{3,0},{4,5},{5,6},{6,7},{7,4},{8,9},{9,10},{10,1... | collective-permute-start | bytes 307208 | tf_op jit(solution)/shard_map/ppermute | solution.py:406
  14.8 6.1 %copy-start.15 = (bf16[400,128]{1,0:T(8,128)(2,1)}, bf16[400,128]{1,0:T(8,128)(2,1)S(1)}, u32[]{:S(2)}) copy-start(bf16[400,128]{1,0:T(8,128)(2,1)S(1)} %collective-permute-done.2.p3) | copy-start | bytes 307204
  20.5 0.6 copy-start.16
  20.9 0.6 copy-start.17
  21.5 22.4 %copy-start.11 = (bf16[784,128]{1,0:T(8,128)(2,1)S(1)}, bf16[784,128]{1,0:T(8,128)(2,1)}, u32[]{:S(2)}) copy-start(bf16[784,128]{1,0:T(8,128)(2,1)} %get-tuple-element.42) | copy-start | bytes 602116
  21.5 23.4 %copy-start.10 = (bf16[784,128]{1,0:T(8,128)(2,1)S(1)}, bf16[784,128]{1,0:T(8,128)(2,1)}, u32[]{:S(2)}) copy-start(bf16[784,128]{1,0:T(8,128)(2,1)} %get-tuple-element.43) | copy-start | bytes 602116
  21.5 27.0 %copy-start.9 = (bf16[784,128]{1,0:T(8,128)(2,1)S(1)}, bf16[784,128]{1,0:T(8,128)(2,1)}, u32[]{:S(2)}) copy-start(bf16[784,128]{1,0:T(8,128)(2,1)} %get-tuple-element.44) | copy-start | bytes 602116
  28.8 5.5 %collective-permute-start.3 = (bf16[208,128]{1,0:T(8,128)(2,1)}, bf16[208,128]{1,0:T(8,128)(2,1)S(1)}, u32[]{:S(2)}, u32[]{:S(2)}) collective-permute-start(bf16[208,128]{1,0:T(8,128)(2,1)} %get-tuple-element.39.a), channel_id=1, source_target_pairs={{0,8},{4,12},{8,0},{12,4},{16,24},{20,28},{24,16},{28,20},{32,40},... | collective-permute-start | bytes 159752 | tf_op jit(solution)/shard_map/ppermute | solution.py:426
  32.0 5.5 %collective-permute-start.5 = (bf16[208,128]{1,0:T(8,128)(2,1)}, bf16[208,128]{1,0:T(8,128)(2,1)S(1)}, u32[]{:S(2)}, u32[]{:S(2)}) collective-permute-start(bf16[208,128]{1,0:T(8,128)(2,1)} %get-tuple-element.40), channel_id=1, source_target_pairs={{0,12},{4,8},{8,4},{12,0},{16,28},{20,24},{24,20},{28,16},{32,44},... | collective-permute-start | bytes 159752 | tf_op jit(solution)/shard_map/ppermute | solution.py:428
  34.3 3.2 %collective-permute-start.4 = (bf16[208,128]{1,0:T(8,128)(2,1)}, bf16[208,128]{1,0:T(8,128)(2,1)S(1)}, u32[]{:S(2)}, u32[]{:S(2)}) collective-permute-start(bf16[208,128]{1,0:T(8,128)(2,1)} %get-tuple-element.40), channel_id=1, source_target_pairs={{0,4},{4,0},{8,12},{12,8},{16,20},{20,16},{24,28},{28,24},{32,36},... | collective-permute-start | bytes 159752 | tf_op jit(solution)/shard_map/ppermute | solution.py:427
  34.3 3.2 %copy-start.3 = (bf16[208,128]{1,0:T(8,128)(2,1)}, bf16[208,128]{1,0:T(8,128)(2,1)S(1)}, u32[]{:S(2)}) copy-start(bf16[208,128]{1,0:T(8,128)(2,1)S(1)} %collective-permute-done.3.b) | copy-start | bytes 159748
  37.5 0.6 copy-start.4
  38.1 0.6 copy-start.5
  40.3 8.2 %collective-permute-start.8 = (bf16[800,128]{1,0:T(8,128)(2,1)}, bf16[800,128]{1,0:T(8,128)(2,1)S(1)}, u32[]{:S(2)}, u32[]{:S(2)}) collective-permute-start(bf16[800,128]{1,0:T(8,128)(2,1)} %merge.1), channel_id=1, source_target_pairs={{0,48},{4,196},{8,56},{12,204},{16,0},{20,212},{24,8},{28,220},{32... | collective-permute-start | bytes 614408 | tf_op jit(solution)/shard_map/ppermute | solution.py:441
  42.9 9.2 %collective-permute-start.7 = (bf16[800,128]{1,0:T(8,128)(2,1)}, bf16[800,128]{1,0:T(8,128)(2,1)S(1)}, u32[]{:S(2)}, u32[]{:S(2)}) collective-permute-start(bf16[800,128]{1,0:T(8,128)(2,1)} %merge.1), channel_id=1, source_target_pairs={{0,32},{4,132},{8,40},{12,140},{16,48},{20,148},{24,56},{28,156},{... | collective-permute-start | bytes 614408 | tf_op jit(solution)/shard_map/ppermute | solution.py:441
  43.2 8.8 %collective-permute-start.6 = (bf16[800,128]{1,0:T(8,128)(2,1)}, bf16[800,128]{1,0:T(8,128)(2,1)S(1)}, u32[]{:S(2)}, u32[]{:S(2)}) collective-permute-start(bf16[800,128]{1,0:T(8,128)(2,1)} %merge.1), channel_id=1, source_target_pairs={{0,16},{4,68},{8,24},{12,76},{16,32},{20,84},{24,40},{28,92},{32,4... | collective-permute-start | bytes 614408 | tf_op jit(solution)/shard_map/ppermute | solution.py:441
  43.9 12.4 %collective-permute-start.12 = (bf16[784,128]{1,0:T(8,128)(2,1)S(1)}, bf16[784,128]{1,0:T(8,128)(2,1)S(1)}, u32[]{:S(2)}, u32[]{:S(2)}) collective-permute-start(bf16[784,128]{1,0:T(8,128)(2,1)S(1)} %copy-done.11), channel_id=1, source_target_pairs={{0,1},{1,2},{2,3},{3,0},{4,5},{5,6},{6,7},{7,4},{8,9},{9,10},{10,1... | collective-permute-start | bytes 602120 | tf_op jit(solution)/shard_map/ppermute | solution.py:406
  45.0 12.4 %collective-permute-start.13 = (bf16[784,128]{1,0:T(8,128)(2,1)S(1)}, bf16[784,128]{1,0:T(8,128)(2,1)S(1)}, u32[]{:S(2)}, u32[]{:S(2)}) collective-permute-start(bf16[784,128]{1,0:T(8,128)(2,1)S(1)} %copy-done.10), channel_id=1, source_target_pairs={{0,2},{1,3},{2,0},{3,1},{4,6},{5,7},{6,4},{7,5},{8,10},{9,11},{10,... | collective-permute-start | bytes 602120 | tf_op jit(solution)/shard_map/ppermute | solution.py:406
  48.5 19.9 %collective-permute-start.14 = (bf16[784,128]{1,0:T(8,128)(2,1)S(1)}, bf16[784,128]{1,0:T(8,128)(2,1)S(1)}, u32[]{:S(2)}, u32[]{:S(2)}) collective-permute-start(bf16[784,128]{1,0:T(8,128)(2,1)S(1)} %copy-done.9), channel_id=1, source_target_pairs={{0,3},{1,0},{2,1},{3,2},{4,7},{5,4},{6,5},{7,6},{8,11},{9,8},{10,9... | collective-permute-start | bytes 602120 | tf_op jit(solution)/shard_map/ppermute | solution.py:406
  53.0 30.1 %copy-start = (bf16[3200,128]{1,0:T(8,128)(2,1)}, bf16[3200,128]{1,0:T(8,128)(2,1)S(1)}, u32[]{:S(2)}) copy-start(bf16[3200,128]{1,0:T(8,128)(2,1)S(1)} %pad_maximum_fusion.refs_0_) | copy-start | bytes 2457604
  53.0 56.0 %copy-start.2 = (bf16[384,192]{0,1:T(8,128)(2,1)S(1)}, bf16[384,192]{0,1:T(8,128)(2,1)}, u32[]{:S(2)}) copy-start(bf16[384,192]{0,1:T(8,128)(2,1)} %param.24) | copy-start | bytes 442372
  53.0 62.6 %collective-permute-start.11 = (bf16[3200,128]{1,0:T(8,128)(2,1)S(1)}, bf16[3200,128]{1,0:T(8,128)(2,1)S(1)}, u32[]{:S(2)}, u32[]{:S(2)}) collective-permute-start(bf16[3200,128]{1,0:T(8,128)(2,1)S(1)} %pad_maximum_fusion.refs_0_), channel_id=1, source_target_pairs={{0,192},{4,52},{8,200},{12,60},{16,208},{20,4},{24,216},{28,12},{3... | collective-permute-start | bytes 2457608 | tf_op jit(solution)/shard_map/ppermute | solution.py:443
  55.8 59.8 %collective-permute-start.10 = (bf16[3200,128]{1,0:T(8,128)(2,1)S(1)}, bf16[3200,128]{1,0:T(8,128)(2,1)S(1)}, u32[]{:S(2)}, u32[]{:S(2)}) collective-permute-start(bf16[3200,128]{1,0:T(8,128)(2,1)S(1)} %pad_maximum_fusion.refs_0_), channel_id=1, source_target_pairs={{0,128},{4,36},{8,136},{12,44},{16,144},{20,52},{24,152},{28,60},{... | collective-permute-start | bytes 2457608 | tf_op jit(solution)/shard_map/ppermute | solution.py:443
  56.3 12.1 %copy-start.12 = (bf16[784,128]{1,0:T(8,128)(2,1)}, bf16[784,128]{1,0:T(8,128)(2,1)S(1)}, u32[]{:S(2)}) copy-start(bf16[784,128]{1,0:T(8,128)(2,1)S(1)} %collective-permute-done.12.p1) | copy-start | bytes 602116
  56.3 59.3 %collective-permute-start.9 = (bf16[3200,128]{1,0:T(8,128)(2,1)S(1)}, bf16[3200,128]{1,0:T(8,128)(2,1)S(1)}, u32[]{:S(2)}, u32[]{:S(2)}) collective-permute-start(bf16[3200,128]{1,0:T(8,128)(2,1)S(1)} %pad_maximum_fusion.refs_0_), channel_id=1, source_target_pairs={{0,64},{4,20},{8,72},{12,28},{16,80},{20,36},{24,88},{28,44},{32,9... | collective-permute-start | bytes 2457608 | tf_op jit(solution)/shard_map/ppermute | solution.py:443
  57.4 11.1 %copy-start.13 = (bf16[784,128]{1,0:T(8,128)(2,1)}, bf16[784,128]{1,0:T(8,128)(2,1)S(1)}, u32[]{:S(2)}) copy-start(bf16[784,128]{1,0:T(8,128)(2,1)S(1)} %collective-permute-done.13.p2) | copy-start | bytes 602116
  68.4 0.7 copy-start.14
  83.1 7.2 %collective-permute-start.15 = (bf16[384,128]{1,0:T(8,128)(2,1)}, bf16[384,128]{1,0:T(8,128)(2,1)S(1)}, u32[]{:S(2)}, u32[]{:S(2)}) collective-permute-start(bf16[384,128]{1,0:T(8,128)(2,1)} %get-tuple-element.46), channel_id=1, source_target_pairs={{0,3},{1,0},{2,1},{3,2},{4,7},{5,4},{6,5},{7,6},{8,11},{9,8},{10,9... | collective-permute-start | bytes 294920 | tf_op jit(solution)/shard_map/ppermute | solution.py:462
  86.0 7.7 %collective-permute-start.16 = (bf16[384,128]{1,0:T(8,128)(2,1)}, bf16[384,128]{1,0:T(8,128)(2,1)}, u32[]{:S(2)}, u32[]{:S(2)}) collective-permute-start(bf16[384,128]{1,0:T(8,128)(2,1)} %get-tuple-element.47), channel_id=1, source_target_pairs={{0,2},{1,3},{2,0},{3,1},{4,6},{5,7},{6,4},{7,5},{8,10},{9,11},{10,... | collective-permute-start | bytes 294920 | tf_op jit(solution)/shard_map/ppermute | solution.py:462
  90.4 25.3 %copy-start.18 = (bf16[384,128]{1,0:T(8,128)(2,1)}, bf16[384,128]{1,0:T(8,128)(2,1)S(1)}, u32[]{:S(2)}) copy-start(bf16[384,128]{1,0:T(8,128)(2,1)S(1)} %collective-permute-done.15.refs_5_) | copy-start | bytes 294916
  90.4 5.9 %collective-permute-start.17 = (bf16[384,128]{1,0:T(8,128)(2,1)}, bf16[384,128]{1,0:T(8,128)(2,1)}, u32[]{:S(2)}, u32[]{:S(2)}) collective-permute-start(bf16[384,128]{1,0:T(8,128)(2,1)} %get-tuple-element.48), channel_id=1, source_target_pairs={{0,1},{1,2},{2,3},{3,0},{4,5},{5,6},{6,7},{7,4},{8,9},{9,10},{10,1... | collective-permute-start | bytes 294920 | tf_op jit(solution)/shard_map/ppermute | solution.py:462
  93.7 6.7 %collective-permute-start.18 = (bf16[384,128]{1,0:T(8,128)(2,1)}, bf16[384,128]{1,0:T(8,128)(2,1)}, u32[]{:S(2)}, u32[]{:S(2)}) collective-permute-start(bf16[384,128]{1,0:T(8,128)(2,1)} %get-tuple-element.49), channel_id=1, source_target_pairs={{0,4},{1,5},{2,6},{3,7},{4,0},{5,1},{6,2},{7,3},{8,12},{9,13},{10,... | collective-permute-start | bytes 294920 | tf_op jit(solution)/shard_map/ppermute | solution.py:462
  96.3 10.8 %collective-permute-start.19 = (bf16[384,128]{1,0:T(8,128)(2,1)}, bf16[384,128]{1,0:T(8,128)(2,1)}, u32[]{:S(2)}, u32[]{:S(2)}) collective-permute-start(bf16[384,128]{1,0:T(8,128)(2,1)} %get-tuple-element.50), channel_id=1, source_target_pairs={{0,7},{1,4},{2,5},{3,6},{4,3},{5,0},{6,1},{7,2},{8,15},{9,12},{10,... | collective-permute-start | bytes 294920 | tf_op jit(solution)/shard_map/ppermute | solution.py:462
  100.4 9.5 %collective-permute-start.20 = (bf16[384,128]{1,0:T(8,128)(2,1)}, bf16[384,128]{1,0:T(8,128)(2,1)}, u32[]{:S(2)}, u32[]{:S(2)}) collective-permute-start(bf16[384,128]{1,0:T(8,128)(2,1)} %get-tuple-element.51), channel_id=1, source_target_pairs={{0,6},{1,7},{2,4},{3,5},{4,2},{5,3},{6,0},{7,1},{8,14},{9,15},{10,... | collective-permute-start | bytes 294920 | tf_op jit(solution)/shard_map/ppermute | solution.py:462
  107.1 8.5 %collective-permute-start.21 = (bf16[384,128]{1,0:T(8,128)(2,1)}, bf16[384,128]{1,0:T(8,128)(2,1)}, u32[]{:S(2)}, u32[]{:S(2)}) collective-permute-start(bf16[384,128]{1,0:T(8,128)(2,1)} %get-tuple-element.52), channel_id=1, source_target_pairs={{0,5},{1,6},{2,7},{3,4},{4,1},{5,2},{6,3},{7,0},{8,13},{9,14},{10,... | collective-permute-start | bytes 294920 | tf_op jit(solution)/shard_map/ppermute | solution.py:462
  115.6 0.9 copy-start.6
  115.6 1.2 copy-start.7
  115.6 1.4 copy-start.8
  154.2 2.0 %collective-permute-start.22 = (bf16[1536,128]{1,0:T(8,128)(2,1)}, bf16[1536,128]{1,0:T(8,128)(2,1)S(1)}, u32[]{:S(2)}, u32[]{:S(2)}) collective-permute-start(bf16[1536,128]{1,0:T(8,128)(2,1)} %get-tuple-element.54), channel_id=1, source_target_pairs={{0,4},{4,0},{8,12},{12,8},{16,20},{20,16},{24,28},{28,24},{32,36},... | collective-permute-start | bytes 1179656 | tf_op jit(solution)/shard_map/ppermute | solution.py:489
  156.1 0.7 copy-start.1
